TPU v7x, 256 devices: a whole 4x4x8 slice. The times are simulated.
256 devices in a mesh: gx: 16 (over z, core), gy: 16 (over y, x).
Axes of the slice: x: 4, y: 4, z: 8, core: 2. Of those that a mesh axis runs over, the one named last changes fastest.
Arguments:
- density: float32 [1024, 512, 128], P('gx', 'gy'), may hold values from -5 to 5
Outputs:
- potential: float32 [1024, 512, 128], P('gx', 'gy')
- residual: float32 [1024, 512, 128], P('gx', 'gy')
All inputs are finite; a program needn't handle non-finite values.
Results may differ from a plain program's by a relative error of at most 0.0004.
Values sent between devices are 32-bit elements; how exact they have to be, the bound alone decides.
A program may use at most 192 MiB of HBM per device.

v0:
```python
import math

import jax
import jax.numpy as jnp
from jax import lax
from jax.sharding import PartitionSpec as P

LEVELS = 4
JACOBI = 20


FOUR_PI = 4.0 * math.pi
WEIGHT_FIRST = 1.0 / (1.25 + 0.75 * math.cos(math.pi / 4.0))
WEIGHT_SECOND = 1.0 / (1.25 - 0.75 * math.cos(math.pi / 4.0))
JACOBI_WEIGHT = 0.8


def extended(cells, sides, width):
    for axis, dim in sides:
        count = lax.axis_size(axis)
        ends = count - 1
        head = lax.slice_in_dim(cells, 0, width, axis=dim)
        tail = lax.slice_in_dim(cells, cells.shape[dim] - width, cells.shape[dim], axis=dim)
        cells = jnp.concatenate(
            [
                lax.ppermute(tail, axis, [(i, (i + 1) % count) for i in range(ends)]),
                cells,
                lax.ppermute(head, axis, [((i + 1) % count, i) for i in range(ends)]),
            ],
            axis=dim,
        )
    return cells


def stencil(padded, inverse):
    beside_all = jnp.pad(padded, ((0, 0), (0, 0), (1, 1)))
    center = beside_all[1:-1, 1:-1, 1:-1]
    total = beside_all[2:, 1:-1, 1:-1] + beside_all[:-2, 1:-1, 1:-1]
    total = total + beside_all[1:-1, 2:, 1:-1] + beside_all[1:-1, :-2, 1:-1]
    total = total + beside_all[1:-1, 1:-1, 2:] + beside_all[1:-1, 1:-1, :-2]
    return (6.0 * center - total) * inverse


def pre_halo(field):
    return extended(field, (("gx", 0), ("gy", 1)), 1)


def post_halo(field):
    return extended(field, (("gx", 0), ("gy", 1)), 1)


def restrict(field):
    sizex, sizey, sizez = field.shape
    return field.reshape(sizex // 2, 2, sizey // 2, 2, sizez // 2, 2).mean(axis=(1, 3, 5))


def prolong(field):
    sizex, sizey, sizez = field.shape
    wide = jnp.broadcast_to(field[:, None, :, None, :, None], (sizex, 2, sizey, 2, sizez, 2))
    return wide.reshape(2 * sizex, 2 * sizey, 2 * sizez)


def on_device(density):
    source = FOUR_PI * density
    sources = []
    smoothed = []
    top = LEVELS
    for current in range(top):
        inverse = 0.25**current
        scale_first = WEIGHT_FIRST * 4.0**current / 6.0
        scale_second = WEIGHT_SECOND * 4.0**current / 6.0
        first = scale_first * source
        second = first + scale_second * (source - stencil(pre_halo(first), inverse))
        remains = source - stencil(pre_halo(second), inverse)
        sources.append(source)
        smoothed.append(second)
        source = restrict(remains)
    coarse_scale = JACOBI_WEIGHT * 4.0**LEVELS / 6.0
    coarse_inverse = 0.25**LEVELS

    def sweep_local(count, field):
        padded = extended(field, (("gx", 0), ("gy", 1)), 1)
        return field + coarse_scale * (source - stencil(padded, coarse_inverse))

    correction = lax.fori_loop(0, JACOBI, sweep_local, jnp.zeros_like(source))
    for current in reversed(range(top)):
        inverse = 0.25**current
        scale_first = WEIGHT_FIRST * 4.0**current / 6.0
        scale_second = WEIGHT_SECOND * 4.0**current / 6.0
        target = sources[current]
        field = smoothed[current] + prolong(correction)
        field = field + scale_first * (target - stencil(post_halo(field), inverse))
        field = field + scale_second * (target - stencil(post_halo(field), inverse))
        correction = field
    residual = sources[0] - stencil(post_halo(correction), 1.0)
    return (correction, residual)


def solution(mesh):
    in_specs = (P("gx", "gy", None),)
    out_specs = (P("gx", "gy", None), P("gx", "gy", None))
    return jax.shard_map(
        on_device, mesh=mesh, in_specs=in_specs, out_specs=out_specs, check_vma=False
    )
```

profile of v0, /device:TPU:152, one launch (start us, length us, event | category | flops | bytes accessed | tf_op | source)
XLA Modules:
  0.0 868.3 jit_solution(16827745261389223125)
XLA Ops:
  10.4 4.8 collective-permute-start.6
  17.2 6.0 collective-permute-done.7
  35.3 3.9 collective-permute-start.11
  39.2 4.0 collective-permute-done.11
  45.2 68.4 %reshape.32 = f32[32,2,16,2,64,2]{5,4,3,2,1,0:T(8,128)} reshape(f32[64,32,128]{2,1,0:T(8,128)S(1)} %fusion.28) | data formatting | bytes 2097152 | tf_op jit(solution)/shard_map/reshape | solution.py:54
  113.6 20.8 %reduce_sum.36 = f32[32,16,64]{2,1,0:T(8,128)S(1)} reduce(f32[32,2,16,2,64,2]{5,4,3,2,1,0:T(8,128)} %reshape.32, f32[]{:T(128)} %constant.69.clone.1), dimensions={1,3,5}, to_apply=%region_0.1 | reduce | flops 229376 | bytes 1179652 | tf_op jit(solution)/shard_map/reduce_sum | solution.py:54
  144.5 3.9 collective-permute-start.15
  162.9 3.9 collective-permute-start.19
  171.1 10.1 %reshape.33 = f32[16,2,8,2,32,2]{5,4,3,2,1,0:T(8,128)} reshape(f32[32,16,64]{2,1,0:T(8,128)S(1)} %fusion.58) | data formatting | bytes 262144 | tf_op jit(solution)/shard_map/reshape | solution.py:54
  181.2 4.1 reduce_sum.37
  195.3 3.9 collective-permute-start.23
  213.2 3.9 collective-permute-start.27
  234.1 3.9 collective-permute-start.31
  251.9 4.1 collective-permute-start.35
  260.0 355.3 %while.13 = (s32[]{:T(128)}, f32[4,2,8]{2,1,0:T(2,128)S(1)}, f32[4,2,8]{2,1,0:T(2,128)S(1)}, s32[]{:T(128)}, s32[]{:T(128)}) while((s32[]{:T(128)}, f32[4,2,8]{2,1,0:T(2,128)S(1)}, f32[4,2,8]{2,1,0:T(2,128)S(1)}, s32[]{:T(128)}, s32[]{:T(128)}) %tuple.75), condition=%wide.region_5.6_spmd.clone, body=%wide.region_4.5_spmd.clone.sunk | while | flops 4355 | bytes 8103 | solution.py:85
  270.0 3.9 collective-permute-start.3
  287.7 3.9 collective-permute-start.3
  305.5 3.9 collective-permute-start.3
  323.3 3.9 collective-permute-start.3
  341.0 3.9 collective-permute-start.3
  358.8 3.9 collective-permute-start.3
  376.6 3.9 collective-permute-start.3
  394.3 3.9 collective-permute-start.3
  412.1 3.9 collective-permute-start.3
  429.9 3.9 collective-permute-start.3
  447.6 3.9 collective-permute-start.3
  465.4 3.9 collective-permute-start.3
  483.2 3.9 collective-permute-start.3
  500.9 3.9 collective-permute-start.3
  518.7 3.9 collective-permute-start.3
  536.4 3.9 collective-permute-start.3
  554.2 3.9 collective-permute-start.3
  572.0 3.9 collective-permute-start.3
  589.7 3.9 collective-permute-start.3
  607.5 3.9 collective-permute-start.3
  625.5 3.9 collective-permute-start.39
  643.3 3.9 collective-permute-start.43
  663.9 3.9 collective-permute-start.47
  681.9 3.9 collective-permute-start.51
  689.8 4.0 broadcast_in_dim.13
  693.8 8.2 reshape.38
  712.0 3.9 collective-permute-start.55
  730.4 3.9 collective-permute-start.59
  738.6 21.5 %broadcast_in_dim.14 = f32[32,2,16,2,64,2]{5,4,3,2,1,0:T(8,128)} broadcast(f32[32,16,64]{2,1,0:T(8,128)S(1)} %fusion.44), dimensions={0,2,4} | broadcast | bytes 1179648 | tf_op jit(solution)/shard_map/broadcast_in_dim | solution.py:59
  760.1 46.8 %reshape.39 = f32[64,32,128]{2,1,0:T(8,128)S(1)} reshape(f32[32,2,16,2,64,2]{5,4,3,2,1,0:T(8,128)} %broadcast_in_dim.14) | data formatting | bytes 2097152 | tf_op jit(solution)/shard_map/reshape | solution.py:60
  821.3 4.0 collective-permute-done.63
  837.4 4.1 collective-permute-start.67
  861.4 4.0 collective-permute-done.71
  (470 shorter events, 524.8 us)
Async XLA Ops:
  4.1 6.3 collective-permute-start.5
  10.4 6.8 collective-permute-start.6
  15.2 7.9 collective-permute-start.7
  27.0 6.3 collective-permute-start.9
  35.3 7.9 collective-permute-start.11
  136.4 6.2 collective-permute-start.13
  144.5 7.8 collective-permute-start.15
  154.7 6.2 collective-permute-start.17
  162.9 7.8 collective-permute-start.19
  195.3 7.7 collective-permute-start.23
  213.2 7.7 collective-permute-start.27
  234.1 7.6 collective-permute-start.31
  251.9 7.6 collective-permute-start.35
  270.0 7.6 collective-permute-start.3
  287.7 7.6 collective-permute-start.3
  305.5 7.6 collective-permute-start.3
  323.3 7.6 collective-permute-start.3
  341.0 7.6 collective-permute-start.3
  358.8 7.6 collective-permute-start.3
  376.6 7.6 collective-permute-start.3
  394.3 7.6 collective-permute-start.3
  412.1 7.6 collective-permute-start.3
  429.9 7.6 collective-permute-start.3
  447.6 7.6 collective-permute-start.3
  465.4 7.6 collective-permute-start.3
  483.2 7.6 collective-permute-start.3
  500.9 7.6 collective-permute-start.3
  518.7 7.6 collective-permute-start.3
  536.4 7.6 collective-permute-start.3
  554.2 7.6 collective-permute-start.3
  572.0 7.6 collective-permute-start.3
  589.7 7.6 collective-permute-start.3
  607.5 7.6 collective-permute-start.3
  625.5 7.6 collective-permute-start.39
  643.3 7.6 collective-permute-start.43
  663.9 7.7 collective-permute-start.47
  673.8 6.1 collective-permute-start.49
  681.9 7.7 collective-permute-start.51
  703.9 6.2 collective-permute-start.53
  712.0 7.8 collective-permute-start.55
  722.2 6.2 collective-permute-start.57
  730.4 7.8 collective-permute-start.59
  809.1 6.3 collective-permute-start.61
  817.4 7.9 collective-permute-start.63
  829.2 6.3 collective-permute-start.65
  837.4 7.9 collective-permute-start.67
  849.2 6.3 collective-permute-start.69
  857.5 7.9 collective-permute-start.71
  (102 other events, 580.4 us)
where the time goes:
time: 873 us; the launch traced here: 868 us
  starting transfers between devices  378 us (43%)
  waiting for transfers between devices  277 us (32%)
  local copies, waits for them, and re-layouts  164 us (19%)
  other arithmetic  46.4 us (5%)
    ppermute x74, waiting for transfers between devices, extended(): lax.ppermute(tail, axis, [(i, (i + 1) % count) for i in range(ends)])  277 us
    ppermute x74, starting transfers between devices, extended(): lax.ppermute(tail, axis, [(i, (i + 1) % count) for i in range(ends)])  233 us
    ppermute x74, starting transfers between devices, extended(): lax.ppermute(head, axis, [((i + 1) % count, i) for i in range(ends)])  145 us
    reshape x4, local copies, waits for them, and re-layouts, restrict(): field.reshape(sizex // 2, 2, sizey // 2, 2, sizez // 2, 2)  80.1 us
    reshape x4, local copies, waits for them, and re-layouts, prolong(): return wide.reshape(2 * sizex, 2 * sizey, 2 * sizez)  56.7 us
    broadcast_in_dim x4, local copies, waits for them, and re-layouts, prolong(): jnp.broadcast_to(field[:, None, :, None, :, None], (sizex, 2, sizey, 2, s...  26.7 us
    reduce_sum x4, other arithmetic, restrict(): field.reshape(sizex // 2, 2, sizey // 2, 2, sizez // 2, 2)  26.3 us
  transfers between devices with their start and end apart: 148, of which 74 were waited for; matrix products, arithmetic and copies ran while one was open for 0% of the time, Pallas kernels for 0%

commit v1 on v0

v1 whole, which is shorter than its diff:
```python
import functools
import math

import jax
import jax.numpy as jnp
from jax import lax
from jax.experimental import pallas as pl
from jax.experimental.pallas import tpu as pltpu
from jax.sharding import PartitionSpec as P

LEVELS = 4
JACOBI = 20
FOUR_PI = 4.0 * math.pi
WEIGHT_FIRST = 1.0 / (1.25 + 0.75 * math.cos(math.pi / 4.0))
WEIGHT_SECOND = 1.0 / (1.25 - 0.75 * math.cos(math.pi / 4.0))
JACOBI_WEIGHT = 0.8

N = 16
LANES = 128
BX = (64, 32, 16, 8, 4)
BY = (32, 16, 8, 4, 2)
OX = (4, 6, 6, 6)
OY = 8
ROWS = (72, 44, 28, 20)
COLS = (48, 32, 24, 24)
START = 4
WIDE = (40, 24, 16, 16)
SPREAD = (0, 1, 2, 2)
HALO = 5
HALO0 = 4
MESH = pl.DeviceIdType.MESH

AROUND = [(dx, dy) for dx in (-1, 0, 1) for dy in (-1, 0, 1) if (dx, dy) != (0, 0)]
AROUND3 = [(dx, dy) for dx in (-1, 0, 1) for dy in (-2, -1, 0, 1, 2) if (dx, dy) != (0, 0)]
PARTNERS = {1: AROUND, 2: AROUND, 3: AROUND3}
EVERYONE = sorted(
    {(dx % N, dy % N) for dx, dy in AROUND3}
    | {(d, 0) for d in range(1, N)}
    | {(0, d) for d in range(1, N)}
)

KINDS = ["own", "ownx", "b", "x", "f", "e"]
SINGLE = [
    "pairs",
    "packer",
    "spreader",
    "cells4",
    "part4",
    "gathery",
    "strip",
    "gatherx",
    "b4",
    "e4",
    "e4wide",
    "out_pot",
    "out_res",
    "load_sem",
    "out_sem",
    "halo_send",
    "halo_recv",
    "part_send",
    "part_recv",
    "gy_send",
    "gy_recv",
    "gx_send",
    "gx_recv",
]


def overlap(step, block, spread):
    low = max(-spread, step * block - HALO)
    high = min(block + spread, step * block + block + HALO)
    return low, high - low, low - step * block


def lanes_of(shape):
    return lax.broadcasted_iota(jnp.int32, shape, len(shape) - 1)


def along_z(cells, level):
    step = 1 << level
    axis = cells.ndim - 1
    lane = lanes_of(cells.shape)
    below = jnp.where(lane >= step, pltpu.roll(cells, step, axis), 0.0)
    above = jnp.where(lane < LANES - step, pltpu.roll(cells, LANES - step, axis), 0.0)
    return below + above


def pair_z(cells, level):
    step = 1 << level
    axis = cells.ndim - 1
    odd = (lanes_of(cells.shape) >> level) & 1
    other = jnp.where(odd == 0, pltpu.roll(cells, LANES - step, axis), pltpu.roll(cells, step, axis))
    return cells + other


def around(ref, row, count, level, start, wide):
    tall = ref[pl.ds(row - 1, count + 2), start : start + wide, :]
    center = tall[1 : count + 1]
    total = tall[:count] + tall[2:]
    total = total + ref[pl.ds(row, count), start - 1 : start - 1 + wide, :]
    total = total + ref[pl.ds(row, count), start + 1 : start + 1 + wide, :]
    return center, total + along_z(center, level)


def chunks(first, count, size, body):
    assert count % size == 0
    if count == size:
        body(first)
        return

    def step(index, carry):
        body(first + index * size)
        return carry

    lax.fori_loop(0, count // size, step, 0)


def kernel(density, potential, residual, *scratch):
    names = [kind + str(level) for kind in KINDS for level in range(LEVELS)] + SINGLE
    refs = dict(zip(names, scratch))
    inbox = dict(zip([(k, d) for k in (1, 2, 3) for d in PARTNERS[k]], scratch[len(names) :]))
    own = [refs[f"own{k}"] for k in range(4)]
    ownx = [refs[f"ownx{k}"] for k in range(4)]
    b = [refs[f"b{k}"] for k in range(4)]
    x = [refs[f"x{k}"] for k in range(4)]
    f = [refs[f"f{k}"] for k in range(4)]
    e = [refs[f"e{k}"] for k in range(4)]
    pairs, packer, spreader = refs["pairs"], refs["packer"], refs["spreader"]

    gx, gy = lax.axis_index("gx"), lax.axis_index("gy")

    def device(step):
        return {"gx": lax.rem(gx + step[0] + N, N), "gy": lax.rem(gy + step[1] + N, N)}

    barrier = pltpu.get_barrier_semaphore()
    for step in EVERYONE:
        pl.semaphore_signal(barrier, inc=1, device_id=device(step), device_id_type=MESH)

    loads = [
        pltpu.make_async_copy(density, own[0].at[4:68, 8:40, :], refs["load_sem"].at[0]),
        pltpu.make_async_copy(density, b[0].at[4:68, 8:40, :], refs["load_sem"].at[1]),
    ]
    for copy in loads:
        copy.start()

    def zero(ref, rows, cols):
        ref[rows[0] : rows[1], cols[0] : cols[1], :] = jnp.zeros(
            (rows[1] - rows[0], cols[1] - cols[0], LANES), jnp.float32
        )

    for ref in (own[0], ownx[0]):
        zero(ref, (0, 4), (0, 48))
        zero(ref, (68, 72), (0, 48))
        zero(ref, (4, 68), (0, 8))
        zero(ref, (4, 68), (40, 48))
    for level in (1, 2, 3):
        zero(own[level], (0, ROWS[level]), (0, COLS[level]))
        zero(ownx[level], (0, ROWS[level]), (0, COLS[level]))
        zero(b[level], (0, ROWS[level]), (0, COLS[level]))
    row = lax.broadcasted_iota(jnp.int32, (768, LANES), 0)
    col = lax.broadcasted_iota(jnp.int32, (768, LANES), 1)
    hit = ((row & 7) == 0) & (((row >> 4) & 7) == (col & 7)) & ((row >> 7) == (col >> 3))
    packer[...] = jnp.where(hit, 0.125, 0.0)
    row = lax.broadcasted_iota(jnp.int32, (LANES, 768), 0)
    col = lax.broadcasted_iota(jnp.int32, (LANES, 768), 1)
    hit = ((row >> 3) == (col >> 7)) & ((row & 7) == ((col >> 4) & 7))
    spreader[...] = jnp.where(hit, 1.0, 0.0)

    def inside_y(level, start, wide):
        place = lax.broadcasted_iota(jnp.int32, (wide, LANES), 0) + (start - OY) + gy * BY[level]
        return jnp.where((place >= 0) & (place < N * BY[level]), 1.0, 0.0)

    left = jnp.where(gx > 0, 1.0, 0.0)
    right = jnp.where(gx < N - 1, 1.0, 0.0)

    def clip_x(ref, level, halo, start, wide):
        first = OX[level]
        last = first + BX[level]
        ref[first - halo : first, start : start + wide, :] *= left
        ref[last : last + halo, start : start + wide, :] *= right

    def presmooth(source, out, level, halo, size):
        inverse = 0.25**level
        scale_first = WEIGHT_FIRST * 4.0**level / 6.0
        scale_second = WEIGHT_SECOND * 4.0**level / 6.0
        linear = scale_first + scale_second
        mixed = scale_first * scale_second * inverse
        start, wide = START, WIDE[level]
        inside = inside_y(level, start, wide)

        def body(row):
            center, total = around(source, row, size, level, start, wide)
            out[pl.ds(row, size), start : start + wide, :] = (
                (linear - 6.0 * mixed) * center + mixed * total
            ) * inside
        chunks(OX[level] - halo, BX[level] + 2 * halo, size, body)
        clip_x(out, level, halo, start, wide)

    def down(source, field, out, level, first, count, size):
        inverse = 0.25**level
        start, wide = START, WIDE[level]
        half = wide // 2

        def body(coarse):
            row = OX[level] + 2 * coarse
            center, total = around(field, row, 2 * size, level, start, wide)
            rest = source[pl.ds(row, 2 * size), start : start + wide, :] - inverse * (6.0 * center - total)
            rest = rest.reshape(size, 2, wide, LANES)
            pairs[:size, :wide, :] = rest[:, 0] + rest[:, 1]
            both = pairs[:size, pl.ds(0, half, stride=2), :] + pairs[:size, pl.ds(1, half, stride=2), :]
            out(coarse, both, size)

        chunks(first, count, size, body)

    def store_level(level):
        start, wide = OY - 2, WIDE[level - 1] // 2
        inside = inside_y(level, start, wide)

        def out(coarse, both, size):
            own[level][pl.ds(OX[level] + coarse, size), start : start + wide, :] = (
                0.125 * pair_z(both, level - 1) * inside
            )
        return out

    loads[0].wait()
    presmooth(own[0], ownx[0], 0, 1, 6)

    pl.semaphore_wait(barrier, len(EVERYONE))

    def halo_copy(index):
        dx, dy = AROUND[index]
        rows = {1: (BX[0] - HALO0, HALO0, 0), 0: (0, BX[0], HALO0), -1: (0, HALO0, BX[0] + HALO0)}[dx]
        cols = {1: (BY[0] - HALO0, HALO0, OY - HALO0), 0: (0, BY[0], OY), -1: (0, HALO0, OY + BY[0])}[dy]
        return pltpu.make_async_remote_copy(
            src_ref=density.at[rows[0] : rows[0] + rows[1], cols[0] : cols[0] + cols[1], :],
            dst_ref=b[0].at[rows[2] : rows[2] + rows[1], cols[2] : cols[2] + cols[1], :],
            send_sem=refs["halo_send"].at[index],
            recv_sem=refs["halo_recv"].at[index],
            device_id=device((dx, dy)),
            device_id_type=MESH,
        )

    halos = [halo_copy(index) for index in range(len(AROUND))]
    for copy in halos:
        copy.start()

    down(own[0], ownx[0], store_level(1), 0, -1, 34, 2)
    clip_x(own[1], 1, SPREAD[1], OY - 2, WIDE[0] // 2)
    presmooth(own[1], ownx[1], 1, 2, 4)
    down(own[1], ownx[1], store_level(2), 1, -2, 20, 2)
    clip_x(own[2], 2, SPREAD[2], OY - 2, WIDE[1] // 2)
    presmooth(own[2], ownx[2], 2, 3, 11)
    down(own[2], ownx[2], store_level(3), 2, -2, 12, 4)
    clip_x(own[3], 3, SPREAD[3], OY - 2, WIDE[2] // 2)
    presmooth(own[3], ownx[3], 3, 3, 14)

    def store_cells(coarse, both, size):
        for index in range(size):
            refs["cells4"][8 * index : 8 * index + 8, :] = both[index]

    down(own[3], ownx[3], store_cells, 3, -2, 8, 8)
    part = jnp.zeros((8, LANES), jnp.float32)
    for place in range(6):
        part = part + jnp.dot(
            refs["cells4"][pl.ds(place, 8, stride=8), :],
            packer[place * LANES : (place + 1) * LANES, :],
            precision=lax.Precision.HIGHEST,
            preferred_element_type=jnp.float32,
        )
    place_x = lax.broadcasted_iota(jnp.int32, (8, LANES), 0) - 2 + gx * BX[4]
    place_y = (lanes_of((8, LANES)) >> 3) - 2 + gy * BY[4]
    inside = (place_x >= 0) & (place_x < N * BX[4]) & (place_y >= 0) & (place_y < N * BY[4])
    part = jnp.where(inside, part, 0.0)
    refs["part4"][...] = part

    def line_copy(axis, step, slot):
        source, slots = (refs["part4"], refs["gathery"]) if axis == "gy" else (refs["strip"], refs["gatherx"])
        return pltpu.make_async_remote_copy(
            src_ref=source,
            dst_ref=slots.at[slot],
            send_sem=refs[axis + "_send"].at[step],
            recv_sem=refs[axis + "_recv"].at[slot],
            device_id=device((step, 0) if axis == "gx" else (0, step)),
            device_id_type=MESH,
        )

    sent = list(halos)
    for step in range(1, N):
        copy = line_copy("gy", step, gy)
        copy.start()
        sent.append(copy)

    parts = {}
    for index, (level, step) in enumerate([(k, d) for k in (3, 2, 1) for d in PARTNERS[k]]):
        low_x, many_x, _ = overlap(step[0], BX[level], SPREAD[level])
        low_y, many_y, _ = overlap(step[1], BY[level], SPREAD[level])
        copy = pltpu.make_async_remote_copy(
            src_ref=own[level].at[
                OX[level] + low_x : OX[level] + low_x + many_x, OY + low_y : OY + low_y + many_y, :
            ],
            dst_ref=inbox[level, step],
            send_sem=refs["part_send"].at[index],
            recv_sem=refs["part_recv"].at[index],
            device_id=device(step),
            device_id_type=MESH,
        )
        copy.start()
        parts[level, step] = copy
        sent.append(copy)

    loads[1].wait()
    for copy in halos:
        copy.wait_recv()
    b[0][0:4, 4:44, :] *= left
    b[0][68:72, 4:44, :] *= right
    for start in (0, 40):
        inside = inside_y(0, start, 8)

        def clip_y(row, start=start, inside=inside):
            b[0][pl.ds(row, 8), start : start + 8, :] *= inside
        chunks(0, 72, 8, clip_y)
    presmooth(b[0], x[0], 0, 3, 5)

    for step in range(1, N):
        slot = lax.rem(gy + N - step, N)
        line_copy("gy", step, slot).wait_recv()
    refs["gathery"][gy] = refs["part4"][...]
    lane = lanes_of((8, LANES))
    near = jnp.zeros((8, LANES), jnp.float32)
    far = jnp.zeros((8, LANES), jnp.float32)
    for slot in range(N):
        moved = pltpu.roll(refs["gathery"][slot], (16 * slot - 16) % LANES, 1)
        if slot < 7:
            near = near + moved
        elif slot > 8:
            far = far + moved
        else:
            low = jnp.where(lane >= 64, moved, 0.0)
            near = near + low
            far = far + (moved - low)
    refs["strip"][0:8, :] = near
    refs["strip"][8:16, :] = far
    for step in range(1, N):
        copy = line_copy("gx", step, gx)
        copy.start()
        sent.append(copy)

    for level in (3, 2, 1):
        spread = SPREAD[level]
        first_x, first_y = OX[level], OY
        rows = slice(first_x - spread, first_x + BX[level] + spread)
        cols = slice(first_y - spread, first_y + BY[level] + spread)
        b[level][rows, cols, :] = own[level][rows, cols, :]
        for step in PARTNERS[level]:
            parts[level, step].wait_recv()
            _, many_x, to_x = overlap(step[0], BX[level], spread)
            _, many_y, to_y = overlap(step[1], BY[level], spread)
            b[level][
                first_x + to_x : first_x + to_x + many_x, first_y + to_y : first_y + to_y + many_y, :
            ] += inbox[level, step][...]
        cover = BY[level] + 2 * HALO
        inside = inside_y(level, OY - HALO, cover)
        b[level][:, OY - HALO : OY - HALO + cover, :] *= inside
        clip_x(b[level], level, HALO, OY - HALO, cover)
        presmooth(b[level], x[level], level, 4, {3: 8, 2: 8, 1: 4}[level])

    for step in range(1, N):
        slot = lax.rem(gx + N - step, N)
        line_copy("gx", step, slot).wait_recv()
    refs["gatherx"][gx] = refs["strip"][...]
    b4, e4 = refs["b4"], refs["e4"]
    b4[...] = jnp.zeros((160, LANES), jnp.float32)
    e4[...] = jnp.zeros((160, LANES), jnp.float32)
    for slot in range(N):
        for tile in range(2):
            at = 80 * tile + 6 + 4 * slot
            b4[at : at + 8, :] += refs["gatherx"][slot, 8 * tile : 8 * tile + 8, :]

    scale = JACOBI_WEIGHT * 4.0**LEVELS / 6.0
    lane = lanes_of((64, LANES))
    for tile in range(2):
        at = 80 * tile + 8
        b4[at : at + 64, :] *= scale
        e4[at : at + 64, :] = b4[at : at + 64, :]

    def sweep(count, carry):
        tiles = [e4[80 * tile + 8 : 80 * tile + 72, :] for tile in range(2)]
        after = [pltpu.roll(tile, 8, 1) for tile in tiles]
        before = [pltpu.roll(tile, LANES - 8, 1) for tile in tiles]
        beside_y = [
            jnp.where(lane >= 8, after[0], 0.0) + jnp.where(lane < LANES - 8, before[0], before[1]),
            jnp.where(lane >= 8, after[1], after[0]) + jnp.where(lane < LANES - 8, before[1], 0.0),
        ]
        new = []
        for tile in range(2):
            at = 80 * tile + 8
            total = e4[at - 1 : at + 63, :] + e4[at + 1 : at + 65, :] + beside_y[tile]
            total = total + jnp.where((lane & 7) != 0, pltpu.roll(tiles[tile], 1, 1), 0.0)
            total = total + jnp.where((lane & 7) != 7, pltpu.roll(tiles[tile], LANES - 1, 1), 0.0)
            new.append(
                (1.0 - JACOBI_WEIGHT) * tiles[tile] + b4[at : at + 64, :] + (JACOBI_WEIGHT / 6.0) * total
            )
        for tile in range(2):
            e4[80 * tile + 8 : 80 * tile + 72, :] = new[tile]
        return carry

    lax.fori_loop(0, JACOBI - 1, sweep, 0)

    lane = lanes_of((8, LANES))
    back = lax.rem(16 - 16 * gy + 2 * LANES, LANES)
    place = lane + 16 * gy - 16
    near = pltpu.roll(e4[pl.ds(6 + 4 * gx, 8), :], back, 1)
    far = pltpu.roll(e4[pl.ds(86 + 4 * gx, 8), :], back, 1)
    mine = jnp.where((place >= 0) & (place < LANES), near, 0.0)
    mine = jnp.where((place >= LANES) & (place < 2 * LANES), far, mine)
    wide4 = jnp.dot(
        mine, spreader[...], precision=lax.Precision.HIGHEST, preferred_element_type=jnp.float32
    )
    for place in range(6):
        refs["e4wide"][pl.ds(place, 8, stride=8), :] = wide4[:, place * LANES : (place + 1) * LANES]

    def correct(level, first, count, size):
        half = 6 if level == 3 else WIDE[level] // 2

        def body(coarse):
            if level == 3:
                fix = refs["e4wide"][...].reshape(8, 8, LANES)[:, :half]
            else:
                fix = e[level + 1][pl.ds(OX[level + 1] + coarse, size), OY - 2 : OY - 2 + half, :]
            fix = jnp.broadcast_to(fix[:, None], (size, 2, half, LANES)).reshape(2 * size, half, LANES)
            row = OX[level] + 2 * coarse
            for parity in range(2):
                place = (pl.ds(row, 2 * size), pl.ds(START + parity, half, stride=2), slice(None))
                x[level][place] = x[level][place] + fix
        chunks(first, count, size, body)

    def relax(field, out, level, weight, halo, size):
        scale_now = weight * 4.0**level / 6.0
        start, wide = START, WIDE[level]
        inside = inside_y(level, start, wide)

        def body(row):
            center, total = around(field, row, size, level, start, wide)
            source = b[level][pl.ds(row, size), start : start + wide, :]
            out[pl.ds(row, size), start : start + wide, :] = (
                (1.0 - weight) * center + scale_now * source + (weight / 6.0) * total
            ) * inside
        chunks(OX[level] - halo, BX[level] + 2 * halo, size, body)
        clip_x(out, level, halo, start, wide)

    correct(3, -2, 8, 8)
    relax(x[3], f[3], 3, WEIGHT_FIRST, 3, 14)
    relax(f[3], e[3], 3, WEIGHT_SECOND, 2, 12)
    correct(2, -2, 12, 6)
    relax(x[2], f[2], 2, WEIGHT_FIRST, 3, 11)
    relax(f[2], e[2], 2, WEIGHT_SECOND, 2, 10)
    correct(1, -2, 20, 4)
    relax(x[1], f[1], 1, WEIGHT_FIRST, 4, 4)
    relax(f[1], e[1], 1, WEIGHT_SECOND, 2, 4)
    correct(0, -2, 36, 4)
    relax(x[0], f[0], 0, WEIGHT_FIRST, 2, 4)
    relax(f[0], e[0], 0, WEIGHT_SECOND, 1, 6)

    def finish(row):
        center, total = around(e[0], row, 4, 0, OY, BY[0])
        source = b[0][pl.ds(row, 4), OY : OY + BY[0], :]
        refs["out_pot"][pl.ds(row - 4, 4)] = FOUR_PI * center
        refs["out_res"][pl.ds(row - 4, 4)] = FOUR_PI * (source - 6.0 * center + total)

    stores = []
    for quarter in range(4):
        chunks(4 + 16 * quarter, 16, 4, finish)
        for index, (source, target) in enumerate(
            ((refs["out_pot"], potential), (refs["out_res"], residual))
        ):
            rows = pl.ds(16 * quarter, 16)
            copy = pltpu.make_async_copy(source.at[rows], target.at[rows], refs["out_sem"].at[index, quarter])
            copy.start()
            stores.append(copy)

    for copy in sent:
        copy.wait_send()
    for copy in stores:
        copy.wait()


def on_device(density):
    def cells(*shape):
        return pltpu.VMEM(shape + (LANES,), jnp.float32)

    level_arrays = [cells(ROWS[k], COLS[k]) for k in range(4)]
    dma = pltpu.SemaphoreType.DMA
    scratch = level_arrays * 6 + [
        cells(8, 40),
        cells(768),
        pltpu.VMEM((LANES, 768), jnp.float32),
        cells(64),
        cells(8),
        cells(N, 8),
        cells(16),
        cells(N, 16),
        cells(160),
        cells(160),
        cells(64),
        cells(64, 32),
        cells(64, 32),
        dma((2,)),
        dma((2, 4)),
        dma((8,)),
        dma((8,)),
        dma((30,)),
        dma((30,)),
        dma((N,)),
        dma((N,)),
        dma((N,)),
        dma((N,)),
    ]
    for level in (1, 2, 3):
        for step in PARTNERS[level]:
            many_x = overlap(step[0], BX[level], SPREAD[level])[1]
            many_y = overlap(step[1], BY[level], SPREAD[level])[1]
            scratch.append(cells(many_x, many_y))
    return pl.pallas_call(
        kernel,
        out_shape=[jax.ShapeDtypeStruct(density.shape, jnp.float32)] * 2,
        in_specs=[pl.BlockSpec(memory_space=pl.ANY)],
        out_specs=[pl.BlockSpec(memory_space=pl.ANY)] * 2,
        scratch_shapes=scratch,
        compiler_params=pltpu.CompilerParams(
            collective_id=0, has_side_effects=True, vmem_limit_bytes=48 * 2**20
        ),
        name="vcycle",
    )(density)


def solution(mesh):
    return jax.shard_map(
        on_device,
        mesh=mesh,
        in_specs=(P("gx", "gy", None),),
        out_specs=(P("gx", "gy", None), P("gx", "gy", None)),
        check_vma=False,
    )
```

time: 873 us -> 50.4 us (0.06)
  the two profiles are of different devices: /device:TPU:152 before, /device:TPU:1 now
where the time goes in v1:
time: 50.4 us; the launch traced here: 50.3 us
  Pallas kernels  46.5 us (92%)
  local copies, waits for them, and re-layouts  3.16 us (6%)
  between operations  0.65 us (1%)
    pallas_call x1, Pallas kernels, on_device(): pl.pallas_call(kernel, out_shape=[jax.ShapeDtypeStruct(density.shape, jnp...  46.5 us
    unnamed x4, local copies, waits for them, and re-layouts  3.16 us

profile of v1, /device:TPU:1, one launch (start us, length us, event | category | flops | bytes accessed | tf_op | source)
XLA Modules:
  0.0 50.3 jit_solution(12427876523738197108)
XLA Ops:
  0.6 0.0 copy-start
  0.6 1.2 %copy-done = f32[64,32,128]{2,1,0:T(8,128)S(1)} copy-done((f32[64,32,128]{2,1,0:T(8,128)S(1)}, f32[64,32,128]{2,1,0:T(8,128)}, u32[]{:S(2)}) %copy-start) | copy-done | bytes 1048600
  1.9 46.5 %vcycle.1 = (f32[64,32,128]{2,1,0:T(8,128)S(1)}, f32[64,32,128]{2,1,0:T(8,128)S(1)}) custom-call(f32[64,32,128]{2,1,0:T(8,128)S(1)} %copy-done), custom_call_target="tpu_custom_call" | custom-call | tf_op jit(solution)/shard_map/vcycle/pallas_call | solution.py:524
  48.4 1.0 %copy.5 = f32[64,32,128]{2,1,0:T(8,128)} copy(f32[64,32,128]{2,1,0:T(8,128)S(1)} %get-tuple-element.4) | data formatting | bytes 2097152
  49.3 1.0 %copy.6 = f32[64,32,128]{2,1,0:T(8,128)} copy(f32[64,32,128]{2,1,0:T(8,128)S(1)} %get-tuple-element.5) | data formatting | bytes 2097152
Async XLA Ops:
  0.6 1.2 %copy-start = (f32[64,32,128]{2,1,0:T(8,128)S(1)}, f32[64,32,128]{2,1,0:T(8,128)}, u32[]{:S(2)}) copy-start(f32[64,32,128]{2,1,0:T(8,128)} %density.1) | copy-start | bytes 3145732

commit v2 on v1

--- a/solution.py
+++ b/solution.py
@@ -105,15 +105,8 @@
 
 def chunks(first, count, size, body):
     assert count % size == 0
-    if count == size:
-        body(first)
-        return
-
-    def step(index, carry):
+    for index in range(count // size):
         body(first + index * size)
-        return carry
-
-    lax.fori_loop(0, count // size, step, 0)
 
 
 def kernel(density, potential, residual, *scratch):

time: 50.4 us -> 40.3 us (0.80)
  Pallas kernels: 46.5 us -> 36.4 us
    pallas_call x1, Pallas kernels: 46.5 us -> 36.4 us  [on_device(): pl.pallas_call(kernel, out_shape=[jax.ShapeDtypeStruct(density.shape, jnp...]
where the time goes in v2:
time: 40.3 us; the launch traced here: 40.2 us
  Pallas kernels  36.4 us (90%)
  local copies, waits for them, and re-layouts  3.16 us (8%)
  between operations  0.65 us (2%)
    pallas_call x1, Pallas kernels, on_device(): pl.pallas_call(kernel, out_shape=[jax.ShapeDtypeStruct(density.shape, jnp...  36.4 us
    unnamed x4, local copies, waits for them, and re-layouts  3.16 us

profile of v2, /device:TPU:1, one launch (start us, length us, event | category | flops | bytes accessed | tf_op | source)
XLA Modules:
  0.0 40.2 jit_solution(654833186851966343)
XLA Ops:
  0.6 0.0 copy-start
  0.6 1.2 %copy-done = f32[64,32,128]{2,1,0:T(8,128)S(1)} copy-done((f32[64,32,128]{2,1,0:T(8,128)S(1)}, f32[64,32,128]{2,1,0:T(8,128)}, u32[]{:S(2)}) %copy-start) | copy-done | bytes 1048600
  1.9 36.4 %vcycle.1 = (f32[64,32,128]{2,1,0:T(8,128)S(1)}, f32[64,32,128]{2,1,0:T(8,128)S(1)}) custom-call(f32[64,32,128]{2,1,0:T(8,128)S(1)} %copy-done), custom_call_target="tpu_custom_call" | custom-call | tf_op jit(solution)/shard_map/vcycle/pallas_call | solution.py:517
  38.2 1.0 %copy.5 = f32[64,32,128]{2,1,0:T(8,128)} copy(f32[64,32,128]{2,1,0:T(8,128)S(1)} %get-tuple-element.4) | data formatting | bytes 2097152
  39.2 1.0 %copy.6 = f32[64,32,128]{2,1,0:T(8,128)} copy(f32[64,32,128]{2,1,0:T(8,128)S(1)} %get-tuple-element.5) | data formatting | bytes 2097152
Async XLA Ops:
  0.6 1.2 %copy-start = (f32[64,32,128]{2,1,0:T(8,128)S(1)}, f32[64,32,128]{2,1,0:T(8,128)}, u32[]{:S(2)}) copy-start(f32[64,32,128]{2,1,0:T(8,128)} %density.1) | copy-start | bytes 3145732

commit v3 on v2

--- a/solution.py
+++ b/solution.py
@@ -1,4 +1,3 @@
-import functools
 import math
 
 import jax
@@ -50,12 +49,11 @@
     "strip",
     "gatherx",
     "b4",
-    "e4",
     "e4wide",
-    "out_pot",
-    "out_res",
+    "sines_x",
+    "sines_yz",
+    "gains",
     "load_sem",
-    "out_sem",
     "halo_send",
     "halo_recv",
     "part_send",
@@ -67,6 +65,73 @@
 ]
 
 
+def sine_table(row, col, count):
+    period = 2.0 * (count + 1)
+    turns = (row + 1.0) * (col + 1.0)
+    turns = turns - period * jnp.floor((turns + 0.5) * (1.0 / period))
+    turns = turns - (count + 1.0)
+    size = jnp.abs(turns)
+    size = jnp.minimum(size, (count + 1.0) - size)
+    angle = size * (math.pi / (count + 1))
+    square = angle * angle
+    total = 1.0
+    for order in (12, 10, 8, 6, 4, 2):
+        total = 1.0 - total * square * (1.0 / (order * (order + 1)))
+    value = angle * total * math.sqrt(2.0 / (count + 1))
+    return jnp.where(turns < 0.0, value, -value)
+
+
+def coarse_tables(sines_x, sines_yz, gains):
+    def places(shape):
+        return [lax.broadcasted_iota(jnp.int32, shape, axis) for axis in range(2)]
+
+    def real(numbers):
+        return numbers.astype(jnp.float32)
+
+    row, col = places((80, LANES))
+    inside = (row >= 8) & (row < 72) & (col < 64)
+    sines_x[...] = jnp.where(inside, sine_table(real(row - 8), real(col), 64), 0.0)
+    for tile in range(8):
+        row, col = places((32, 256))
+        row = row + 32 * tile
+        sines_yz[32 * tile : 32 * tile + 32, :] = sine_table(
+            real(row >> 3), real(col >> 3), 32
+        ) * sine_table(real(row & 7), real(col & 7), 8)
+
+    def value(place, count):
+        sine = sine_table(real(place), jnp.zeros(place.shape, jnp.float32), 2 * count + 1)
+        return (4.0 * (count + 1)) * sine * sine
+
+    row, col = places((64, 256))
+    damped = (JACOBI_WEIGHT / 6.0) * (value(row, 64) + value(col >> 3, 32) + value(col & 7, 8))
+    kept = 1.0 - damped
+    power = kept * kept
+    power = power * power
+    fourth = power
+    power = power * power
+    power = power * power * fourth
+    assert JACOBI == 20
+    gains[...] = (JACOBI_WEIGHT * 4.0**LEVELS / 6.0) * (1.0 - power) / damped
+
+
+def ring(step, count):
+    return min(step % count, -step % count)
+
+
+def hops_x(step):
+    return sum(ring((core + step) // 2 - core // 2, 8) for core in range(2))
+
+
+def hops_y(step):
+    return sum(ring((x + step) // 4, 4) + ring((x + step) % 4 - x, 4) for x in range(4))
+
+
+FAR_FIRST = {
+    "gx": sorted(range(1, N), key=hops_x, reverse=True),
+    "gy": sorted(range(1, N), key=hops_y, reverse=True),
+}
+
+
 def overlap(step, block, spread):
     low = max(-spread, step * block - HALO)
     high = min(block + spread, step * block + block + HALO)
@@ -103,13 +168,27 @@
     return center, total + along_z(center, level)
 
 
+def inside_y(level, start, wide, scale=1.0):
+    place = lax.broadcasted_iota(jnp.int32, (wide, LANES), 0) + (start - OY)
+    place = place + lax.axis_index("gy") * BY[level]
+    return jnp.where((place >= 0) & (place < N * BY[level]), scale, 0.0)
+
+
+def clip_x(ref, level, halo, start, wide):
+    gx = lax.axis_index("gx")
+    first = OX[level]
+    last = first + BX[level]
+    ref[first - halo : first, start : start + wide, :] *= jnp.where(gx > 0, 1.0, 0.0)
+    ref[last : last + halo, start : start + wide, :] *= jnp.where(gx < N - 1, 1.0, 0.0)
+
+
 def chunks(first, count, size, body):
     assert count % size == 0
     for index in range(count // size):
         body(first + index * size)
 
 
-def kernel(density, potential, residual, *scratch):
+def kernel(density, e1_out, relaxed_low, relaxed_high, source_low, source_high, *scratch):
     names = [kind + str(level) for kind in KINDS for level in range(LEVELS)] + SINGLE
     refs = dict(zip(names, scratch))
     inbox = dict(zip([(k, d) for k in (1, 2, 3) for d in PARTNERS[k]], scratch[len(names) :]))
@@ -118,7 +197,7 @@
     b = [refs[f"b{k}"] for k in range(4)]
     x = [refs[f"x{k}"] for k in range(4)]
     f = [refs[f"f{k}"] for k in range(4)]
-    e = [refs[f"e{k}"] for k in range(4)]
+    e = [None, e1_out, refs["e2"], refs["e3"]]
     pairs, packer, spreader = refs["pairs"], refs["packer"], refs["spreader"]
 
     gx, gy = lax.axis_index("gx"), lax.axis_index("gy")
@@ -131,10 +210,15 @@
         pl.semaphore_signal(barrier, inc=1, device_id=device(step), device_id_type=MESH)
 
     loads = [
-        pltpu.make_async_copy(density, own[0].at[4:68, 8:40, :], refs["load_sem"].at[0]),
-        pltpu.make_async_copy(density, b[0].at[4:68, 8:40, :], refs["load_sem"].at[1]),
+        pltpu.make_async_copy(
+            density.at[16 * part : 16 * part + 16],
+            own[0].at[4 + 16 * part : 20 + 16 * part, 8:40, :],
+            refs["load_sem"].at[part],
+        )
+        for part in range(4)
     ]
-    for copy in loads:
+    later = pltpu.make_async_copy(density, b[0].at[4:68, 8:40, :], refs["load_sem"].at[4])
+    for copy in loads + [later]:
         copy.start()
 
     def zero(ref, rows, cols):
@@ -160,20 +244,7 @@
     hit = ((row >> 3) == (col >> 7)) & ((row & 7) == ((col >> 4) & 7))
     spreader[...] = jnp.where(hit, 1.0, 0.0)
 
-    def inside_y(level, start, wide):
-        place = lax.broadcasted_iota(jnp.int32, (wide, LANES), 0) + (start - OY) + gy * BY[level]
-        return jnp.where((place >= 0) & (place < N * BY[level]), 1.0, 0.0)
-
-    left = jnp.where(gx > 0, 1.0, 0.0)
-    right = jnp.where(gx < N - 1, 1.0, 0.0)
-
-    def clip_x(ref, level, halo, start, wide):
-        first = OX[level]
-        last = first + BX[level]
-        ref[first - halo : first, start : start + wide, :] *= left
-        ref[last : last + halo, start : start + wide, :] *= right
-
-    def presmooth(source, out, level, halo, size):
+    def presmooth(source, out, level, halo, size, ready=None):
         inverse = 0.25**level
         scale_first = WEIGHT_FIRST * 4.0**level / 6.0
         scale_second = WEIGHT_SECOND * 4.0**level / 6.0
@@ -183,6 +254,8 @@
         inside = inside_y(level, start, wide)
 
         def body(row):
+            if ready is not None:
+                ready(row + size)
             center, total = around(source, row, size, level, start, wide)
             out[pl.ds(row, size), start : start + wide, :] = (
                 (linear - 6.0 * mixed) * center + mixed * total
@@ -200,8 +273,9 @@
             center, total = around(field, row, 2 * size, level, start, wide)
             rest = source[pl.ds(row, 2 * size), start : start + wide, :] - inverse * (6.0 * center - total)
             rest = rest.reshape(size, 2, wide, LANES)
-            pairs[:size, :wide, :] = rest[:, 0] + rest[:, 1]
-            both = pairs[:size, pl.ds(0, half, stride=2), :] + pairs[:size, pl.ds(1, half, stride=2), :]
+            at = pl.ds(coarse - first, size)
+            pairs[at, :wide, :] = rest[:, 0] + rest[:, 1]
+            both = pairs[at, pl.ds(0, half, stride=2), :] + pairs[at, pl.ds(1, half, stride=2), :]
             out(coarse, both, size)
 
         chunks(first, count, size, body)
@@ -216,8 +290,13 @@
             )
         return out
 
-    loads[0].wait()
-    presmooth(own[0], ownx[0], 0, 1, 6)
+    waiting = list(loads)
+
+    def loaded(row):
+        while waiting and (row >= 4 + 16 * (4 - len(waiting)) or row >= 67):
+            waiting.pop(0).wait()
+
+    presmooth(own[0], ownx[0], 0, 1, 11, loaded)
 
     pl.semaphore_wait(barrier, len(EVERYONE))
 
@@ -279,7 +358,7 @@
         )
 
     sent = list(halos)
-    for step in range(1, N):
+    for step in FAR_FIRST["gy"]:
         copy = line_copy("gy", step, gy)
         copy.start()
         sent.append(copy)
@@ -302,18 +381,37 @@
         parts[level, step] = copy
         sent.append(copy)
 
-    loads[1].wait()
+    def relax(field, out, level, weight, halo, size, scale=1.0, halves=None):
+        scale_now = weight * 4.0**level / 6.0
+        start, wide = START, WIDE[level]
+        inside = inside_y(level, start, wide, scale)
+
+        def body(row):
+            center, total = around(field, row, size, level, start, wide)
+            source = b[level][pl.ds(row, size), start : start + wide, :]
+            result = ((1.0 - weight) * center + scale_now * source + (weight / 6.0) * total) * inside
+            if halves is None:
+                out[pl.ds(row, size), start : start + wide, :] = result
+            else:
+                first = row - OX[0] + 1
+                halves[first // 33][pl.ds(first % 33, size)] = result
+
+        chunks(OX[level] - halo, BX[level] + 2 * halo, size, body)
+        if halves is None:
+            clip_x(out, level, halo, start, wide)
+
+    later.wait()
     for copy in halos:
         copy.wait_recv()
-    b[0][0:4, 4:44, :] *= left
-    b[0][68:72, 4:44, :] *= right
+    clip_x(b[0], 0, HALO0, START, WIDE[0])
     for start in (0, 40):
         inside = inside_y(0, start, 8)
 
         def clip_y(row, start=start, inside=inside):
             b[0][pl.ds(row, 8), start : start + 8, :] *= inside
         chunks(0, 72, 8, clip_y)
-    presmooth(b[0], x[0], 0, 3, 5)
+    presmooth(b[0], x[0], 0, 3, 7)
+    relax(x[0], f[0], 0, WEIGHT_FIRST, 2, 4)
 
     for step in range(1, N):
         slot = lax.rem(gy + N - step, N)
@@ -334,10 +432,15 @@
             far = far + (moved - low)
     refs["strip"][0:8, :] = near
     refs["strip"][8:16, :] = far
-    for step in range(1, N):
+    for step in FAR_FIRST["gx"]:
         copy = line_copy("gx", step, gx)
         copy.start()
         sent.append(copy)
+
+    relax(f[0], None, 0, WEIGHT_SECOND, 1, 11, FOUR_PI, (relaxed_low, relaxed_high))
+    source_low[...] = FOUR_PI * b[0][4:36, 8:40, :]
+    source_high[...] = FOUR_PI * b[0][36:68, 8:40, :]
+    coarse_tables(refs["sines_x"], refs["sines_yz"], refs["gains"])
 
     for level in (3, 2, 1):
         spread = SPREAD[level]
@@ -362,54 +465,32 @@
         slot = lax.rem(gx + N - step, N)
         line_copy("gx", step, slot).wait_recv()
     refs["gatherx"][gx] = refs["strip"][...]
-    b4, e4 = refs["b4"], refs["e4"]
-    b4[...] = jnp.zeros((160, LANES), jnp.float32)
-    e4[...] = jnp.zeros((160, LANES), jnp.float32)
+    b4 = refs["b4"]
+    b4[...] = jnp.zeros((80, 256), jnp.float32)
     for slot in range(N):
         for tile in range(2):
-            at = 80 * tile + 6 + 4 * slot
-            b4[at : at + 8, :] += refs["gatherx"][slot, 8 * tile : 8 * tile + 8, :]
-
-    scale = JACOBI_WEIGHT * 4.0**LEVELS / 6.0
-    lane = lanes_of((64, LANES))
-    for tile in range(2):
-        at = 80 * tile + 8
-        b4[at : at + 64, :] *= scale
-        e4[at : at + 64, :] = b4[at : at + 64, :]
-
-    def sweep(count, carry):
-        tiles = [e4[80 * tile + 8 : 80 * tile + 72, :] for tile in range(2)]
-        after = [pltpu.roll(tile, 8, 1) for tile in tiles]
-        before = [pltpu.roll(tile, LANES - 8, 1) for tile in tiles]
-        beside_y = [
-            jnp.where(lane >= 8, after[0], 0.0) + jnp.where(lane < LANES - 8, before[0], before[1]),
-            jnp.where(lane >= 8, after[1], after[0]) + jnp.where(lane < LANES - 8, before[1], 0.0),
-        ]
-        new = []
-        for tile in range(2):
-            at = 80 * tile + 8
-            total = e4[at - 1 : at + 63, :] + e4[at + 1 : at + 65, :] + beside_y[tile]
-            total = total + jnp.where((lane & 7) != 0, pltpu.roll(tiles[tile], 1, 1), 0.0)
-            total = total + jnp.where((lane & 7) != 7, pltpu.roll(tiles[tile], LANES - 1, 1), 0.0)
-            new.append(
-                (1.0 - JACOBI_WEIGHT) * tiles[tile] + b4[at : at + 64, :] + (JACOBI_WEIGHT / 6.0) * total
-            )
-        for tile in range(2):
-            e4[80 * tile + 8 : 80 * tile + 72, :] = new[tile]
-        return carry
-
-    lax.fori_loop(0, JACOBI - 1, sweep, 0)
+            at = (slice(6 + 4 * slot, 14 + 4 * slot), slice(LANES * tile, LANES * tile + LANES))
+            b4[at] += refs["gatherx"][slot, 8 * tile : 8 * tile + 8, :]
+
+    def times(one, other):
+        return jnp.dot(
+            one, other, precision=lax.Precision.HIGHEST, preferred_element_type=jnp.float32
+        )
+
+    sines_yz = refs["sines_yz"][...]
+    waves = times(refs["sines_x"][8:72, :64], b4[8:72, :])
+    waves = times(waves, sines_yz) * refs["gains"][...]
+    waves = times(refs["sines_x"][pl.ds(6 + 4 * gx, 8), :64], waves)
+    coarsest = times(waves, sines_yz)
 
     lane = lanes_of((8, LANES))
     back = lax.rem(16 - 16 * gy + 2 * LANES, LANES)
     place = lane + 16 * gy - 16
-    near = pltpu.roll(e4[pl.ds(6 + 4 * gx, 8), :], back, 1)
-    far = pltpu.roll(e4[pl.ds(86 + 4 * gx, 8), :], back, 1)
+    near = pltpu.roll(coarsest[:, :LANES], back, 1)
+    far = pltpu.roll(coarsest[:, LANES:], back, 1)
     mine = jnp.where((place >= 0) & (place < LANES), near, 0.0)
     mine = jnp.where((place >= LANES) & (place < 2 * LANES), far, mine)
-    wide4 = jnp.dot(
-        mine, spreader[...], precision=lax.Precision.HIGHEST, preferred_element_type=jnp.float32
-    )
+    wide4 = times(mine, spreader[...])
     for place in range(6):
         refs["e4wide"][pl.ds(place, 8, stride=8), :] = wide4[:, place * LANES : (place + 1) * LANES]
 
@@ -428,20 +509,6 @@
                 x[level][place] = x[level][place] + fix
         chunks(first, count, size, body)
 
-    def relax(field, out, level, weight, halo, size):
-        scale_now = weight * 4.0**level / 6.0
-        start, wide = START, WIDE[level]
-        inside = inside_y(level, start, wide)
-
-        def body(row):
-            center, total = around(field, row, size, level, start, wide)
-            source = b[level][pl.ds(row, size), start : start + wide, :]
-            out[pl.ds(row, size), start : start + wide, :] = (
-                (1.0 - weight) * center + scale_now * source + (weight / 6.0) * total
-            ) * inside
-        chunks(OX[level] - halo, BX[level] + 2 * halo, size, body)
-        clip_x(out, level, halo, start, wide)
-
     correct(3, -2, 8, 8)
     relax(x[3], f[3], 3, WEIGHT_FIRST, 3, 14)
     relax(f[3], e[3], 3, WEIGHT_SECOND, 2, 12)
@@ -451,29 +518,72 @@
     correct(1, -2, 20, 4)
     relax(x[1], f[1], 1, WEIGHT_FIRST, 4, 4)
     relax(f[1], e[1], 1, WEIGHT_SECOND, 2, 4)
-    correct(0, -2, 36, 4)
-    relax(x[0], f[0], 0, WEIGHT_FIRST, 2, 4)
-    relax(f[0], e[0], 0, WEIGHT_SECOND, 1, 6)
-
-    def finish(row):
-        center, total = around(e[0], row, 4, 0, OY, BY[0])
-        source = b[0][pl.ds(row, 4), OY : OY + BY[0], :]
-        refs["out_pot"][pl.ds(row - 4, 4)] = FOUR_PI * center
-        refs["out_res"][pl.ds(row - 4, 4)] = FOUR_PI * (source - 6.0 * center + total)
-
-    stores = []
-    for quarter in range(4):
-        chunks(4 + 16 * quarter, 16, 4, finish)
-        for index, (source, target) in enumerate(
-            ((refs["out_pot"], potential), (refs["out_res"], residual))
-        ):
-            rows = pl.ds(16 * quarter, 16)
-            copy = pltpu.make_async_copy(source.at[rows], target.at[rows], refs["out_sem"].at[index, quarter])
-            copy.start()
-            stores.append(copy)
 
     for copy in sent:
         copy.wait_send()
+
+
+def finish(
+    e1, relaxed_low, relaxed_high, source_low, source_high, potential, residual, first, pot, out, out_sem
+):
+    relaxed = (relaxed_low, relaxed_high)
+    source = (source_low, source_high)
+
+    inside = inside_y(1, OY - 1, 18, FOUR_PI)
+
+    def spread(coarse):
+        rows = pl.ds(OX[1] + coarse, 17)
+        cells = e1[rows, OY - 1 : OY + 17, :]
+        same = (1.0 - WEIGHT_FIRST * 2.0 / 3.0) * cells + (WEIGHT_FIRST / 6.0) * along_z(cells, 0)
+        same = same * inside
+        share = inside * (WEIGHT_FIRST / 6.0)
+        for odd_x in range(2):
+            beside = e1[pl.ds(OX[1] + coarse + 2 * odd_x - 1, 17), OY - 1 : OY + 17, :]
+            for odd_y in range(2):
+                below = OY - 2 + 2 * odd_y
+                both = beside + e1[rows, below : below + 18, :]
+                both = same + share * both
+                for index in range(17):
+                    row = OX[0] + 2 * (coarse + index) + odd_x
+                    first[row, pl.ds(OY - 2 + odd_y, 18, stride=2), :] = both[index]
+
+    chunks(-1, 34, 17, spread)
+    clip_x(first, 0, 2, START, WIDE[0])
+
+    inside = inside_y(0, START, WIDE[0])
+    cols = slice(START, START + WIDE[0])
+
+    def second(row):
+        center, total = around(first, row, 11, 0, START, WIDE[0])
+        later = (1.0 - WEIGHT_SECOND) * center + (WEIGHT_SECOND / 6.0) * total
+        place = row - OX[0] + 1
+        pot[pl.ds(row, 11), cols, :] = (
+            relaxed[place // 33][pl.ds(place % 33, 11)] + later * inside
+        )
+
+    chunks(OX[0] - 1, BX[0] + 2, 11, second)
+    clip_x(pot, 0, 1, START, WIDE[0])
+
+    stores = []
+
+    def store(origin, target, index, part):
+        copy = pltpu.make_async_copy(
+            origin, target.at[16 * part : 16 * part + 16], out_sem.at[index, part]
+        )
+        copy.start()
+        stores.append(copy)
+
+    for part in range(4):
+        store(pot.at[4 + 16 * part : 20 + 16 * part, OY : OY + BY[0], :], potential, 0, part)
+
+    def rest(row):
+        center, total = around(pot, row, 8, 0, OY, BY[0])
+        place = row - OX[0]
+        out[pl.ds(place, 8)] = source[place // 32][pl.ds(place % 32, 8)] - 6.0 * center + total
+
+    for part in range(4):
+        chunks(4 + 16 * part, 16, 8, rest)
+        store(out.at[16 * part : 16 * part + 16], residual, 1, part)
     for copy in stores:
         copy.wait()
 
@@ -485,7 +595,7 @@
     level_arrays = [cells(ROWS[k], COLS[k]) for k in range(4)]
     dma = pltpu.SemaphoreType.DMA
     scratch = level_arrays * 6 + [
-        cells(8, 40),
+        cells(34, 40),
         cells(768),
         pltpu.VMEM((LANES, 768), jnp.float32),
         cells(64),
@@ -493,13 +603,12 @@
         cells(N, 8),
         cells(16),
         cells(N, 16),
-        cells(160),
-        cells(160),
+        pltpu.VMEM((80, 256), jnp.float32),
         cells(64),
-        cells(64, 32),
-        cells(64, 32),
-        dma((2,)),
-        dma((2, 4)),
+        cells(80),
+        pltpu.VMEM((256, 256), jnp.float32),
+        pltpu.VMEM((64, 256), jnp.float32),
+        dma((5,)),
         dma((8,)),
         dma((8,)),
         dma((30,)),
@@ -514,17 +623,34 @@
             many_x = overlap(step[0], BX[level], SPREAD[level])[1]
             many_y = overlap(step[1], BY[level], SPREAD[level])[1]
             scratch.append(cells(many_x, many_y))
-    return pl.pallas_call(
+    hbm = pl.BlockSpec(memory_space=pltpu.HBM)
+    vmem = pl.BlockSpec(memory_space=pltpu.VMEM)
+    shapes = [(ROWS[1], COLS[1])] + [(33, WIDE[0])] * 2 + [(32, 32)] * 2
+    shared = pl.pallas_call(
         kernel,
-        out_shape=[jax.ShapeDtypeStruct(density.shape, jnp.float32)] * 2,
-        in_specs=[pl.BlockSpec(memory_space=pl.ANY)],
-        out_specs=[pl.BlockSpec(memory_space=pl.ANY)] * 2,
+        out_shape=[jax.ShapeDtypeStruct(shape + (LANES,), jnp.float32) for shape in shapes],
+        in_specs=[hbm],
+        out_specs=[vmem] * 5,
         scratch_shapes=scratch,
         compiler_params=pltpu.CompilerParams(
-            collective_id=0, has_side_effects=True, vmem_limit_bytes=48 * 2**20
+            collective_id=0, has_side_effects=True, vmem_limit_bytes=50 * 2**20 + 2**18
         ),
         name="vcycle",
     )(density)
+    return pl.pallas_call(
+        finish,
+        out_shape=[jax.ShapeDtypeStruct(density.shape, jnp.float32)] * 2,
+        in_specs=[vmem] * 5,
+        out_specs=[hbm] * 2,
+        scratch_shapes=[
+            cells(ROWS[0], COLS[0]),
+            cells(ROWS[0], COLS[0]),
+            cells(64, 32),
+            dma((2, 4)),
+        ],
+        compiler_params=pltpu.CompilerParams(vmem_limit_bytes=24 * 2**20),
+        name="finish",
+    )(*shared)
 
 
 def solution(mesh):

time: 40.3 us -> 35.8 us (0.89)
  local copies, waits for them, and re-layouts: 3.16 us -> 0 us
  Pallas kernels: 36.4 us -> 35.1 us
    unnamed x4 -> x0, local copies, waits for them, and re-layouts: 3.16 us -> none
    pallas_call x1 -> x2, Pallas kernels: 36.4 us -> 35.1 us  [the longest x1 32.4 us: on_device(): pl.pallas_call(kernel, out_shape=[jax.ShapeDtypeStruct(shape + (LANES,),...]
where the time goes in v3:
time: 35.8 us; the launch traced here: 35.7 us
  Pallas kernels  35.1 us (98%)
  between operations  0.64 us (2%)
    pallas_call x1, Pallas kernels, on_device(): pl.pallas_call(kernel, out_shape=[jax.ShapeDtypeStruct(shape + (LANES,),...  32.4 us
    pallas_call x1, Pallas kernels, on_device(): pl.pallas_call(finish, out_shape=[jax.ShapeDtypeStruct(density.shape, jnp...  2.7 us

profile of v3, /device:TPU:1, one launch (start us, length us, event | category | flops | bytes accessed | tf_op | source)
XLA Modules:
  0.0 35.7 jit_solution(3045039003277871052)
XLA Ops:
  0.6 32.4 %vcycle.1 = (f32[44,32,128]{2,1,0:T(8,128)S(1)}, f32[33,40,128]{2,1,0:T(8,128)S(1)}, f32[33,40,128]{2,1,0:T(8,128)S(1)}, f32[32,32,128]{2,1,0:T(8,128)S(1)}, f32[32,32,128]{2,1,0:T(8,128)S(1)}) custom-call(f32[64,32,128]{2,1,0:T(8,128)} %density.1), custom_call_target="tpu_custom_call" | custom-call | tf_op jit(solution)/shard_map/vcycle/pallas_call | solution.py:629
  33.0 2.7 %finish.1 = (f32[64,32,128]{2,1,0:T(8,128)}, f32[64,32,128]{2,1,0:T(8,128)}) custom-call(f32[44,32,128]{2,1,0:T(8,128)S(1)} %get-tuple-element.7.e1, f32[33,40,128]{2,1,0:T(8,128)S(1)} %get-tuple-element.8.relaxed_low, f32[33,40,128]{2,1,0:T(8,128)S(1)} %get-tuple-element.9.relaxed_high, f32[32,32,128]{2,1,0:T(8,128)S(1)} %get-tuple-element.10.source_low, ...), custom_call_target="tpu_custom_call" | custom-call | tf_op jit(solution)/shard_map/finish/pallas_call | solution.py:640

commit v4 on v3

--- a/solution.py
+++ b/solution.py
@@ -26,6 +26,7 @@
 WIDE = (40, 24, 16, 16)
 SPREAD = (0, 1, 2, 2)
 HALO = 5
+GROUP = (1, 2, 4, 4)
 HALO0 = 4
 MESH = pl.DeviceIdType.MESH
 
@@ -53,6 +54,9 @@
     "sines_x",
     "sines_yz",
     "gains",
+    "packed1",
+    "packed2",
+    "packed3",
     "load_sem",
     "halo_send",
     "halo_recv",
@@ -138,6 +142,14 @@
     return low, high - low, low - step * block
 
 
+def groups(step, level):
+    low, many, _ = overlap(step, BX[level], SPREAD[level])
+    low += SPREAD[level]
+    first = low // GROUP[level]
+    last = -(-(low + many) // GROUP[level])
+    return first, last - first, low - first * GROUP[level]
+
+
 def lanes_of(shape):
     return lax.broadcasted_iota(jnp.int32, shape, len(shape) - 1)
 
@@ -157,6 +169,28 @@
     odd = (lanes_of(cells.shape) >> level) & 1
     other = jnp.where(odd == 0, pltpu.roll(cells, LANES - step, axis), pltpu.roll(cells, step, axis))
     return cells + other
+
+
+def pack(rows, size):
+    count, wide = rows.shape[0] // size, rows.shape[1]
+    rows = rows.reshape(count, size, wide, LANES)
+    which = lanes_of((count, wide, LANES)) & (size - 1)
+    packed = rows[:, size - 1]
+    for index in range(size - 1):
+        packed = jnp.where(which == index, rows[:, index], packed)
+    return packed
+
+
+def unpack(packed, size):
+    lane = lanes_of(packed.shape)
+    rows = [packed]
+    bit = 1
+    while bit < size:
+        even = [jnp.where((lane & bit) == 0, row, pltpu.roll(row, bit, 2)) for row in rows]
+        odd = [jnp.where((lane & bit) == 0, pltpu.roll(row, LANES - bit, 2), row) for row in rows]
+        rows = even + odd
+        bit *= 2
+    return jnp.stack(rows, axis=1).reshape(size * packed.shape[0], packed.shape[1], LANES)
 
 
 def around(ref, row, count, level, start, wide):
@@ -217,8 +251,7 @@
         )
         for part in range(4)
     ]
-    later = pltpu.make_async_copy(density, b[0].at[4:68, 8:40, :], refs["load_sem"].at[4])
-    for copy in loads + [later]:
+    for copy in loads:
         copy.start()
 
     def zero(ref, rows, cols):
@@ -298,14 +331,14 @@
 
     presmooth(own[0], ownx[0], 0, 1, 11, loaded)
 
-    pl.semaphore_wait(barrier, len(EVERYONE))
-
     def halo_copy(index):
         dx, dy = AROUND[index]
         rows = {1: (BX[0] - HALO0, HALO0, 0), 0: (0, BX[0], HALO0), -1: (0, HALO0, BX[0] + HALO0)}[dx]
         cols = {1: (BY[0] - HALO0, HALO0, OY - HALO0), 0: (0, BY[0], OY), -1: (0, HALO0, OY + BY[0])}[dy]
         return pltpu.make_async_remote_copy(
-            src_ref=density.at[rows[0] : rows[0] + rows[1], cols[0] : cols[0] + cols[1], :],
+            src_ref=own[0].at[
+                4 + rows[0] : 4 + rows[0] + rows[1], OY + cols[0] : OY + cols[0] + cols[1], :
+            ],
             dst_ref=b[0].at[rows[2] : rows[2] + rows[1], cols[2] : cols[2] + cols[1], :],
             send_sem=refs["halo_send"].at[index],
             recv_sem=refs["halo_recv"].at[index],
@@ -314,9 +347,9 @@
         )
 
     halos = [halo_copy(index) for index in range(len(AROUND))]
+    pl.semaphore_wait(barrier, len(EVERYONE))
     for copy in halos:
         copy.start()
-
     down(own[0], ownx[0], store_level(1), 0, -1, 34, 2)
     clip_x(own[1], 1, SPREAD[1], OY - 2, WIDE[0] // 2)
     presmooth(own[1], ownx[1], 1, 2, 4)
@@ -364,22 +397,31 @@
         sent.append(copy)
 
     parts = {}
-    for index, (level, step) in enumerate([(k, d) for k in (3, 2, 1) for d in PARTNERS[k]]):
-        low_x, many_x, _ = overlap(step[0], BX[level], SPREAD[level])
-        low_y, many_y, _ = overlap(step[1], BY[level], SPREAD[level])
-        copy = pltpu.make_async_remote_copy(
-            src_ref=own[level].at[
-                OX[level] + low_x : OX[level] + low_x + many_x, OY + low_y : OY + low_y + many_y, :
-            ],
-            dst_ref=inbox[level, step],
-            send_sem=refs["part_send"].at[index],
-            recv_sem=refs["part_recv"].at[index],
-            device_id=device(step),
-            device_id_type=MESH,
-        )
-        copy.start()
-        parts[level, step] = copy
-        sent.append(copy)
+    for level in (3, 2, 1):
+        spread = SPREAD[level]
+        first = OX[level] - spread
+        wide = BY[level] + 2 * spread
+        packed = refs["packed" + str(level)]
+        packed[:, OY : OY + wide, :] = pack(
+            own[level][first : first + BX[level] + 2 * spread, OY - spread : OY - spread + wide, :],
+            GROUP[level],
+        )
+        for step in PARTNERS[level]:
+            index = len(parts)
+            first, count, _ = groups(step[0], level)
+            low_y, many_y, _ = overlap(step[1], BY[level], spread)
+            low_y += OY + spread
+            copy = pltpu.make_async_remote_copy(
+                src_ref=packed.at[first : first + count, low_y : low_y + many_y, :],
+                dst_ref=inbox[level, step],
+                send_sem=refs["part_send"].at[index],
+                recv_sem=refs["part_recv"].at[index],
+                device_id=device(step),
+                device_id_type=MESH,
+            )
+            copy.start()
+            parts[level, step] = copy
+            sent.append(copy)
 
     def relax(field, out, level, weight, halo, size, scale=1.0, halves=None):
         scale_now = weight * 4.0**level / 6.0
@@ -400,7 +442,8 @@
         if halves is None:
             clip_x(out, level, halo, start, wide)
 
-    later.wait()
+    coarse_tables(refs["sines_x"], refs["sines_yz"], refs["gains"])
+    b[0][4:68, 8:40, :] = own[0][4:68, 8:40, :]
     for copy in halos:
         copy.wait_recv()
     clip_x(b[0], 0, HALO0, START, WIDE[0])
@@ -411,7 +454,6 @@
             b[0][pl.ds(row, 8), start : start + 8, :] *= inside
         chunks(0, 72, 8, clip_y)
     presmooth(b[0], x[0], 0, 3, 7)
-    relax(x[0], f[0], 0, WEIGHT_FIRST, 2, 4)
 
     for step in range(1, N):
         slot = lax.rem(gy + N - step, N)
@@ -437,10 +479,10 @@
         copy.start()
         sent.append(copy)
 
+    relax(x[0], f[0], 0, WEIGHT_FIRST, 2, 4)
     relax(f[0], None, 0, WEIGHT_SECOND, 1, 11, FOUR_PI, (relaxed_low, relaxed_high))
     source_low[...] = FOUR_PI * b[0][4:36, 8:40, :]
     source_high[...] = FOUR_PI * b[0][36:68, 8:40, :]
-    coarse_tables(refs["sines_x"], refs["sines_yz"], refs["gains"])
 
     for level in (3, 2, 1):
         spread = SPREAD[level]
@@ -452,9 +494,11 @@
             parts[level, step].wait_recv()
             _, many_x, to_x = overlap(step[0], BX[level], spread)
             _, many_y, to_y = overlap(step[1], BY[level], spread)
+            skip = groups(step[0], level)[2]
+            rows = unpack(inbox[level, step][...], GROUP[level])
             b[level][
                 first_x + to_x : first_x + to_x + many_x, first_y + to_y : first_y + to_y + many_y, :
-            ] += inbox[level, step][...]
+            ] += rows[skip : skip + many_x]
         cover = BY[level] + 2 * HALO
         inside = inside_y(level, OY - HALO, cover)
         b[level][:, OY - HALO : OY - HALO + cover, :] *= inside
@@ -608,7 +652,10 @@
         cells(80),
         pltpu.VMEM((256, 256), jnp.float32),
         pltpu.VMEM((64, 256), jnp.float32),
-        dma((5,)),
+        cells(17, 32),
+        cells(5, 24),
+        cells(3, 24),
+        dma((4,)),
         dma((8,)),
         dma((8,)),
         dma((30,)),
@@ -620,9 +667,8 @@
     ]
     for level in (1, 2, 3):
         for step in PARTNERS[level]:
-            many_x = overlap(step[0], BX[level], SPREAD[level])[1]
             many_y = overlap(step[1], BY[level], SPREAD[level])[1]
-            scratch.append(cells(many_x, many_y))
+            scratch.append(cells(groups(step[0], level)[1], many_y))
     hbm = pl.BlockSpec(memory_space=pltpu.HBM)
     vmem = pl.BlockSpec(memory_space=pltpu.VMEM)
     shapes = [(ROWS[1], COLS[1])] + [(33, WIDE[0])] * 2 + [(32, 32)] * 2

time: 35.8 us -> 32.7 us (0.913)
  Pallas kernels: 35.1 us -> 32 us
    pallas_call x1, Pallas kernels: 32.4 us -> 29.3 us  [on_device(): pl.pallas_call(kernel, out_shape=[jax.ShapeDtypeStruct(shape + (LANES,),...]
where the time goes in v4:
time: 32.7 us; the launch traced here: 32.6 us
  Pallas kernels  32 us (98%)
  between operations  0.64 us (2%)
    pallas_call x1, Pallas kernels, on_device(): pl.pallas_call(kernel, out_shape=[jax.ShapeDtypeStruct(shape + (LANES,),...  29.3 us
    pallas_call x1, Pallas kernels, on_device(): pl.pallas_call(finish, out_shape=[jax.ShapeDtypeStruct(density.shape, jnp...  2.7 us

profile of v4, /device:TPU:1, one launch (start us, length us, event | category | flops | bytes accessed | tf_op | source)
XLA Modules:
  0.0 32.6 jit_solution(17419780483586607689)
XLA Ops:
  0.6 29.3 %vcycle.1 = (f32[44,32,128]{2,1,0:T(8,128)S(1)}, f32[33,40,128]{2,1,0:T(8,128)S(1)}, f32[33,40,128]{2,1,0:T(8,128)S(1)}, f32[32,32,128]{2,1,0:T(8,128)S(1)}, f32[32,32,128]{2,1,0:T(8,128)S(1)}) custom-call(f32[64,32,128]{2,1,0:T(8,128)} %density.1), custom_call_target="tpu_custom_call" | custom-call | tf_op jit(solution)/shard_map/vcycle/pallas_call | solution.py:675
  29.9 2.7 %finish.1 = (f32[64,32,128]{2,1,0:T(8,128)}, f32[64,32,128]{2,1,0:T(8,128)}) custom-call(f32[44,32,128]{2,1,0:T(8,128)S(1)} %get-tuple-element.7.e1, f32[33,40,128]{2,1,0:T(8,128)S(1)} %get-tuple-element.8.relaxed_low, f32[33,40,128]{2,1,0:T(8,128)S(1)} %get-tuple-element.9.relaxed_high, f32[32,32,128]{2,1,0:T(8,128)S(1)} %get-tuple-element.10.source_low, ...), custom_call_target="tpu_custom_call" | custom-call | tf_op jit(solution)/shard_map/finish/pallas_call | solution.py:686

commit v5 on v4

--- a/solution.py
+++ b/solution.py
@@ -27,12 +27,12 @@
 SPREAD = (0, 1, 2, 2)
 HALO = 5
 GROUP = (1, 2, 4, 4)
-HALO0 = 4
+SPREAD0 = 3
 MESH = pl.DeviceIdType.MESH
 
 AROUND = [(dx, dy) for dx in (-1, 0, 1) for dy in (-1, 0, 1) if (dx, dy) != (0, 0)]
 AROUND3 = [(dx, dy) for dx in (-1, 0, 1) for dy in (-2, -1, 0, 1, 2) if (dx, dy) != (0, 0)]
-PARTNERS = {1: AROUND, 2: AROUND, 3: AROUND3}
+PARTNERS = {0: AROUND, 1: AROUND, 2: AROUND, 3: AROUND3}
 EVERYONE = sorted(
     {(dx % N, dy % N) for dx, dy in AROUND3}
     | {(d, 0) for d in range(1, N)}
@@ -225,10 +225,10 @@
 def kernel(density, e1_out, relaxed_low, relaxed_high, source_low, source_high, *scratch):
     names = [kind + str(level) for kind in KINDS for level in range(LEVELS)] + SINGLE
     refs = dict(zip(names, scratch))
-    inbox = dict(zip([(k, d) for k in (1, 2, 3) for d in PARTNERS[k]], scratch[len(names) :]))
+    inbox = dict(zip([(k, d) for k in range(LEVELS) for d in PARTNERS[k]], scratch[len(names) :]))
     own = [refs[f"own{k}"] for k in range(4)]
     ownx = [refs[f"ownx{k}"] for k in range(4)]
-    b = [refs[f"b{k}"] for k in range(4)]
+    b = [own[0]] + [refs[f"b{k}"] for k in (1, 2, 3)]
     x = [refs[f"x{k}"] for k in range(4)]
     f = [refs[f"f{k}"] for k in range(4)]
     e = [None, e1_out, refs["e2"], refs["e3"]]
@@ -264,6 +264,8 @@
         zero(ref, (68, 72), (0, 48))
         zero(ref, (4, 68), (0, 8))
         zero(ref, (4, 68), (40, 48))
+    zero(refs["f0"], (0, 2), (0, 48))
+    zero(refs["f0"], (70, 72), (0, 48))
     for level in (1, 2, 3):
         zero(own[level], (0, ROWS[level]), (0, COLS[level]))
         zero(ownx[level], (0, ROWS[level]), (0, COLS[level]))
@@ -293,6 +295,7 @@
             out[pl.ds(row, size), start : start + wide, :] = (
                 (linear - 6.0 * mixed) * center + mixed * total
             ) * inside
+
         chunks(OX[level] - halo, BX[level] + 2 * halo, size, body)
         clip_x(out, level, halo, start, wide)
 
@@ -331,25 +334,6 @@
 
     presmooth(own[0], ownx[0], 0, 1, 11, loaded)
 
-    def halo_copy(index):
-        dx, dy = AROUND[index]
-        rows = {1: (BX[0] - HALO0, HALO0, 0), 0: (0, BX[0], HALO0), -1: (0, HALO0, BX[0] + HALO0)}[dx]
-        cols = {1: (BY[0] - HALO0, HALO0, OY - HALO0), 0: (0, BY[0], OY), -1: (0, HALO0, OY + BY[0])}[dy]
-        return pltpu.make_async_remote_copy(
-            src_ref=own[0].at[
-                4 + rows[0] : 4 + rows[0] + rows[1], OY + cols[0] : OY + cols[0] + cols[1], :
-            ],
-            dst_ref=b[0].at[rows[2] : rows[2] + rows[1], cols[2] : cols[2] + cols[1], :],
-            send_sem=refs["halo_send"].at[index],
-            recv_sem=refs["halo_recv"].at[index],
-            device_id=device((dx, dy)),
-            device_id_type=MESH,
-        )
-
-    halos = [halo_copy(index) for index in range(len(AROUND))]
-    pl.semaphore_wait(barrier, len(EVERYONE))
-    for copy in halos:
-        copy.start()
     down(own[0], ownx[0], store_level(1), 0, -1, 34, 2)
     clip_x(own[1], 1, SPREAD[1], OY - 2, WIDE[0] // 2)
     presmooth(own[1], ownx[1], 1, 2, 4)
@@ -390,7 +374,8 @@
             device_id_type=MESH,
         )
 
-    sent = list(halos)
+    pl.semaphore_wait(barrier, len(EVERYONE))
+    sent = []
     for step in FAR_FIRST["gy"]:
         copy = line_copy("gy", step, gy)
         copy.start()
@@ -423,7 +408,7 @@
             parts[level, step] = copy
             sent.append(copy)
 
-    def relax(field, out, level, weight, halo, size, scale=1.0, halves=None):
+    def relax(field, out, level, weight, halo, size, scale=1.0):
         scale_now = weight * 4.0**level / 6.0
         start, wide = START, WIDE[level]
         inside = inside_y(level, start, wide, scale)
@@ -432,29 +417,35 @@
             center, total = around(field, row, size, level, start, wide)
             source = b[level][pl.ds(row, size), start : start + wide, :]
             result = ((1.0 - weight) * center + scale_now * source + (weight / 6.0) * total) * inside
-            if halves is None:
-                out[pl.ds(row, size), start : start + wide, :] = result
-            else:
-                first = row - OX[0] + 1
-                halves[first // 33][pl.ds(first % 33, size)] = result
+            out[pl.ds(row, size), start : start + wide, :] = result
 
         chunks(OX[level] - halo, BX[level] + 2 * halo, size, body)
-        if halves is None:
-            clip_x(out, level, halo, start, wide)
+        clip_x(out, level, halo, start, wide)
 
     coarse_tables(refs["sines_x"], refs["sines_yz"], refs["gains"])
-    b[0][4:68, 8:40, :] = own[0][4:68, 8:40, :]
-    for copy in halos:
-        copy.wait_recv()
-    clip_x(b[0], 0, HALO0, START, WIDE[0])
-    for start in (0, 40):
-        inside = inside_y(0, start, 8)
-
-        def clip_y(row, start=start, inside=inside):
-            b[0][pl.ds(row, 8), start : start + 8, :] *= inside
-        chunks(0, 72, 8, clip_y)
-    presmooth(b[0], x[0], 0, 3, 7)
-
+    relax(ownx[0], f[0], 0, WEIGHT_FIRST, 2, 17)
+    relax(f[0], x[0], 0, WEIGHT_SECOND, SPREAD0, 14, FOUR_PI)
+
+    def side(step, block):
+        low = max(-SPREAD0, step * block - 1)
+        high = min(block + SPREAD0, step * block + block + 1)
+        return low, high - low, low - step * block + 1
+
+    strips = []
+    for index, step in enumerate(AROUND):
+        low_x, many_x, _ = side(step[0], BX[0])
+        low_y, many_y, _ = side(step[1], BY[0])
+        copy = pltpu.make_async_remote_copy(
+            src_ref=x[0].at[OX[0] + low_x : OX[0] + low_x + many_x, OY + low_y : OY + low_y + many_y, :],
+            dst_ref=inbox[0, step],
+            send_sem=refs["halo_send"].at[index],
+            recv_sem=refs["halo_recv"].at[index],
+            device_id=device(step),
+            device_id_type=MESH,
+        )
+        copy.start()
+        strips.append(copy)
+        sent.append(copy)
     for step in range(1, N):
         slot = lax.rem(gy + N - step, N)
         line_copy("gy", step, slot).wait_recv()
@@ -479,11 +470,6 @@
         copy.start()
         sent.append(copy)
 
-    relax(x[0], f[0], 0, WEIGHT_FIRST, 2, 4)
-    relax(f[0], None, 0, WEIGHT_SECOND, 1, 11, FOUR_PI, (relaxed_low, relaxed_high))
-    source_low[...] = FOUR_PI * b[0][4:36, 8:40, :]
-    source_high[...] = FOUR_PI * b[0][36:68, 8:40, :]
-
     for level in (3, 2, 1):
         spread = SPREAD[level]
         first_x, first_y = OX[level], OY
@@ -505,6 +491,22 @@
         clip_x(b[level], level, HALO, OY - HALO, cover)
         presmooth(b[level], x[level], level, 4, {3: 8, 2: 8, 1: 4}[level])
 
+    source_low[...] = FOUR_PI * own[0][4:36, 8:40, :]
+    source_high[...] = FOUR_PI * own[0][36:68, 8:40, :]
+    relaxed_low[...] = x[0][3:36, START : START + WIDE[0], :]
+    relaxed_high[...] = x[0][36:69, START : START + WIDE[0], :]
+    for index, step in enumerate(AROUND):
+        strips[index].wait_recv()
+        _, many_x, to_x = side(step[0], BX[0])
+        _, many_y, to_y = side(step[1], BY[0])
+        to_y += OY - 1 - START
+        for half, target in enumerate((relaxed_low, relaxed_high)):
+            low, high = max(to_x, 33 * half), min(to_x + many_x, 33 * half + 33)
+            if low < high:
+                target[low - 33 * half : high - 33 * half, to_y : to_y + many_y, :] += inbox[0, step][
+                    low - to_x : high - to_x
+                ]
+
     for step in range(1, N):
         slot = lax.rem(gx + N - step, N)
         line_copy("gx", step, slot).wait_recv()
@@ -602,32 +604,41 @@
         later = (1.0 - WEIGHT_SECOND) * center + (WEIGHT_SECOND / 6.0) * total
         place = row - OX[0] + 1
         pot[pl.ds(row, 11), cols, :] = (
-            relaxed[place // 33][pl.ds(place % 33, 11)] + later * inside
-        )
-
-    chunks(OX[0] - 1, BX[0] + 2, 11, second)
-    clip_x(pot, 0, 1, START, WIDE[0])
+            relaxed[place // 33][pl.ds(place % 33, 11)] + later
+        ) * inside
+
+    def rest(row, count):
+        center, total = around(pot, row, count, 0, OY, BY[0])
+        place = row - OX[0]
+        for half in range(2):
+            low, high = max(place, 32 * half), min(place + count, 32 * half + 32)
+            if low < high:
+                part = slice(low - place, high - place)
+                here = source[half][low - 32 * half : high - 32 * half]
+                out[low:high] = here - 6.0 * center[part] + total[part]
 
     stores = []
 
-    def store(origin, target, index, part):
+    def store(origin, target, index, low, high):
         copy = pltpu.make_async_copy(
-            origin, target.at[16 * part : 16 * part + 16], out_sem.at[index, part]
+            origin, target.at[low:high], out_sem.at[index, len(stores) // 2]
         )
         copy.start()
         stores.append(copy)
 
-    for part in range(4):
-        store(pot.at[4 + 16 * part : 20 + 16 * part, OY : OY + BY[0], :], potential, 0, part)
-
-    def rest(row):
-        center, total = around(pot, row, 8, 0, OY, BY[0])
-        place = row - OX[0]
-        out[pl.ds(place, 8)] = source[place // 32][pl.ds(place % 32, 8)] - 6.0 * center + total
-
-    for part in range(4):
-        chunks(4 + 16 * part, 16, 8, rest)
-        store(out.at[16 * part : 16 * part + 16], residual, 1, part)
+    done_pot, done_rest = 0, 0
+    for part in range(6):
+        second(OX[0] - 1 + 11 * part)
+        if part == 0:
+            pot[3:4, cols, :] *= jnp.where(lax.axis_index("gx") > 0, 1.0, 0.0)
+        if part == 5:
+            pot[68:69, cols, :] *= jnp.where(lax.axis_index("gx") < N - 1, 1.0, 0.0)
+        ready = 11 * part + 10
+        low, done_pot = done_pot, min(ready, BX[0])
+        store(pot.at[4 + low : 4 + done_pot, OY : OY + BY[0], :], potential, 0, low, done_pot)
+        low, done_rest = done_rest, min(ready - 1, BX[0])
+        rest(OX[0] + low, done_rest - low)
+        store(out.at[low:done_rest], residual, 1, low, done_rest)
     for copy in stores:
         copy.wait()
 
@@ -665,6 +676,8 @@
         dma((N,)),
         dma((N,)),
     ]
+    for dx, dy in AROUND:
+        scratch.append(cells(SPREAD0 + 1 if dx else BX[0] + 2, SPREAD0 + 1 if dy else BY[0] + 2))
     for level in (1, 2, 3):
         for step in PARTNERS[level]:
             many_y = overlap(step[1], BY[level], SPREAD[level])[1]
@@ -692,7 +705,7 @@
             cells(ROWS[0], COLS[0]),
             cells(ROWS[0], COLS[0]),
             cells(64, 32),
-            dma((2, 4)),
+            dma((2, 6)),
         ],
         compiler_params=pltpu.CompilerParams(vmem_limit_bytes=24 * 2**20),
         name="finish",

time: 32.7 us -> 31.4 us (0.960)
  Pallas kernels: 32 us -> 30.7 us
    pallas_call x1, Pallas kernels: 29.3 us -> 27.7 us  [on_device(): pl.pallas_call(kernel, out_shape=[jax.ShapeDtypeStruct(shape + (LANES,),...]
where the time goes in v5:
time: 31.4 us; the launch traced here: 31.3 us
  Pallas kernels  30.7 us (98%)
  between operations  0.64 us (2%)
    pallas_call x1, Pallas kernels, on_device(): pl.pallas_call(kernel, out_shape=[jax.ShapeDtypeStruct(shape + (LANES,),...  27.7 us
    pallas_call x1, Pallas kernels, on_device(): pl.pallas_call(finish, out_shape=[jax.ShapeDtypeStruct(density.shape, jnp...  2.98 us

profile of v5, /device:TPU:1, one launch (start us, length us, event | category | flops | bytes accessed | tf_op | source)
XLA Modules:
  0.0 31.3 jit_solution(744158702932352362)
XLA Ops:
  0.6 27.7 %vcycle.1 = (f32[44,32,128]{2,1,0:T(8,128)S(1)}, f32[33,40,128]{2,1,0:T(8,128)S(1)}, f32[33,40,128]{2,1,0:T(8,128)S(1)}, f32[32,32,128]{2,1,0:T(8,128)S(1)}, f32[32,32,128]{2,1,0:T(8,128)S(1)}) custom-call(f32[64,32,128]{2,1,0:T(8,128)} %density.1), custom_call_target="tpu_custom_call" | custom-call | tf_op jit(solution)/shard_map/vcycle/pallas_call | solution.py:688
  28.4 3.0 %finish.1 = (f32[64,32,128]{2,1,0:T(8,128)}, f32[64,32,128]{2,1,0:T(8,128)}) custom-call(f32[44,32,128]{2,1,0:T(8,128)S(1)} %get-tuple-element.7.e1, f32[33,40,128]{2,1,0:T(8,128)S(1)} %get-tuple-element.8.relaxed_low, f32[33,40,128]{2,1,0:T(8,128)S(1)} %get-tuple-element.9.relaxed_high, f32[32,32,128]{2,1,0:T(8,128)S(1)} %get-tuple-element.10.source_low, ...), custom_call_target="tpu_custom_call" | custom-call | tf_op jit(solution)/shard_map/finish/pallas_call | solution.py:699

commit v6 on v5

--- a/solution.py
+++ b/solution.py
@@ -607,38 +607,29 @@
             relaxed[place // 33][pl.ds(place % 33, 11)] + later
         ) * inside
 
-    def rest(row, count):
-        center, total = around(pot, row, count, 0, OY, BY[0])
-        place = row - OX[0]
-        for half in range(2):
-            low, high = max(place, 32 * half), min(place + count, 32 * half + 32)
-            if low < high:
-                part = slice(low - place, high - place)
-                here = source[half][low - 32 * half : high - 32 * half]
-                out[low:high] = here - 6.0 * center[part] + total[part]
+    chunks(OX[0] - 1, BX[0] + 2, 11, second)
+    clip_x(pot, 0, 1, START, WIDE[0])
 
     stores = []
 
-    def store(origin, target, index, low, high):
+    def store(origin, target, index, part):
         copy = pltpu.make_async_copy(
-            origin, target.at[low:high], out_sem.at[index, len(stores) // 2]
+            origin, target.at[16 * part : 16 * part + 16], out_sem.at[index, part]
         )
         copy.start()
         stores.append(copy)
 
-    done_pot, done_rest = 0, 0
-    for part in range(6):
-        second(OX[0] - 1 + 11 * part)
-        if part == 0:
-            pot[3:4, cols, :] *= jnp.where(lax.axis_index("gx") > 0, 1.0, 0.0)
-        if part == 5:
-            pot[68:69, cols, :] *= jnp.where(lax.axis_index("gx") < N - 1, 1.0, 0.0)
-        ready = 11 * part + 10
-        low, done_pot = done_pot, min(ready, BX[0])
-        store(pot.at[4 + low : 4 + done_pot, OY : OY + BY[0], :], potential, 0, low, done_pot)
-        low, done_rest = done_rest, min(ready - 1, BX[0])
-        rest(OX[0] + low, done_rest - low)
-        store(out.at[low:done_rest], residual, 1, low, done_rest)
+    for part in range(4):
+        store(pot.at[4 + 16 * part : 20 + 16 * part, OY : OY + BY[0], :], potential, 0, part)
+
+    def rest(row):
+        center, total = around(pot, row, 8, 0, OY, BY[0])
+        place = row - OX[0]
+        out[pl.ds(place, 8)] = source[place // 32][pl.ds(place % 32, 8)] - 6.0 * center + total
+
+    for part in range(4):
+        chunks(4 + 16 * part, 16, 8, rest)
+        store(out.at[16 * part : 16 * part + 16], residual, 1, part)
     for copy in stores:
         copy.wait()
 
@@ -705,7 +696,7 @@
             cells(ROWS[0], COLS[0]),
             cells(ROWS[0], COLS[0]),
             cells(64, 32),
-            dma((2, 6)),
+            dma((2, 4)),
         ],
         compiler_params=pltpu.CompilerParams(vmem_limit_bytes=24 * 2**20),
         name="finish",

time: 31.4 us -> 31.2 us (level)
  no operation moved by 1% of the time
where the time goes in v6:
time: 31.2 us; the launch traced here: 31.1 us
  Pallas kernels  30.4 us (97%)
  between operations  0.64 us (2%)
    pallas_call x1, Pallas kernels, on_device(): pl.pallas_call(kernel, out_shape=[jax.ShapeDtypeStruct(shape + (LANES,),...  27.7 us
    pallas_call x1, Pallas kernels, on_device(): pl.pallas_call(finish, out_shape=[jax.ShapeDtypeStruct(density.shape, jnp...  2.7 us

profile of v6, /device:TPU:1, one launch (start us, length us, event | category | flops | bytes accessed | tf_op | source)
XLA Modules:
  0.0 31.1 jit_solution(13694072134204721983)
XLA Ops:
  0.6 27.7 %vcycle.1 = (f32[44,32,128]{2,1,0:T(8,128)S(1)}, f32[33,40,128]{2,1,0:T(8,128)S(1)}, f32[33,40,128]{2,1,0:T(8,128)S(1)}, f32[32,32,128]{2,1,0:T(8,128)S(1)}, f32[32,32,128]{2,1,0:T(8,128)S(1)}) custom-call(f32[64,32,128]{2,1,0:T(8,128)} %density.1), custom_call_target="tpu_custom_call" | custom-call | tf_op jit(solution)/shard_map/vcycle/pallas_call | solution.py:679
  28.4 2.7 %finish.1 = (f32[64,32,128]{2,1,0:T(8,128)}, f32[64,32,128]{2,1,0:T(8,128)}) custom-call(f32[44,32,128]{2,1,0:T(8,128)S(1)} %get-tuple-element.7.e1, f32[33,40,128]{2,1,0:T(8,128)S(1)} %get-tuple-element.8.relaxed_low, f32[33,40,128]{2,1,0:T(8,128)S(1)} %get-tuple-element.9.relaxed_high, f32[32,32,128]{2,1,0:T(8,128)S(1)} %get-tuple-element.10.source_low, ...), custom_call_target="tpu_custom_call" | custom-call | tf_op jit(solution)/shard_map/finish/pallas_call | solution.py:690
